TPU v7x, 32 devices: a whole 2x2x4 slice. The times are simulated.
32 devices in a mesh: groups: 2 (over y), tok: 4 (over z), col: 2 (over x), head: 2 (over core).
Axes of the slice: x: 2, y: 2, z: 4, core: 2. Of those that a mesh axis runs over, the one named last changes fastest.
Arguments:
- latents: bfloat16 [4, 8192, 512], P(('groups', 'col'), ('tok', 'head')), parts along dimension 0, may hold values from -110 to 110
- weights: bfloat16 [2, 512, 32768], P(None, None, ('tok', 'head')), may hold values from -0.25 to 0.25
- start_basis: bfloat16 [32768, 256], P(('tok', 'head')), may hold values from -6 to 6
- layer_pick: int32 [4, 128], P('groups'), parts along dimension 0, may hold values from 0 to 1
Outputs:
- basis: float32 [4, 32768, 256], P(('groups', 'col'), ('tok', 'head')), parts along dimension 0
- core: float32 [4, 512, 256], P(('groups', 'col')), parts along dimension 0
There are 2 independent parts, one for each index of `groups`. A program takes and returns all parts, laid end to end along the dimension named above; an argument that names none is the same for every part. Nothing has to cross between parts.
Inputs may be any that keep to these rules, and one draw needn't show every extreme that they name: `layer_pick`: a layer of the stack for each head of each layer slot.
All inputs are finite; a program needn't handle non-finite values.
Results may differ from a plain program's by a relative error of at most 0.0003.
Values sent between devices are 32-bit elements; how exact they have to be, the bound alone decides.
A program may use at most 128 MiB of HBM per device.

v0:
```python
import math

import jax
import jax.numpy as jnp
from jax import lax
from jax.sharding import PartitionSpec as P

OUT = 32768
STEPS = 2
HEAD_OUT = 256


def product(left, right):
    return jnp.dot(left, right, precision=lax.Precision.HIGHEST)


def right_solve(lower, block):
    return lax.linalg.triangular_solve(lower, block, left_side=False, lower=True, transpose_a=True)


def orthonormal(block):
    lower = jnp.linalg.cholesky(product(block.T, block))
    return right_solve(lower, block)


def summed_gram(outgoing):
    return lax.psum(outgoing, ("tok", "head"))


def on_device(latents, weights, start_basis, layer_pick):
    act = latents[0]
    width = act.shape[1]
    stack_count = weights.shape[0]
    col_count = weights.shape[2]
    heads_here = col_count // HEAD_OUT
    slot = lax.axis_index("col")
    first_head = lax.axis_index(("tok", "head")) * heads_here
    picks = lax.dynamic_slice_in_dim(layer_pick[slot], first_head, heads_here, 0)
    stacked = weights.reshape(stack_count, width, heads_here, HEAD_OUT)
    chosen = stacked[picks, :, jnp.arange(heads_here, dtype=jnp.int32), :]
    weight = jnp.transpose(chosen, (1, 0, 2)).reshape(width, col_count).astype(jnp.float32)
    local_gram = jnp.dot(act.T, act, preferred_element_type=jnp.float32)
    current = start_basis.astype(jnp.float32)
    incoming = summed_gram(local_gram)
    upper = jnp.linalg.cholesky(incoming).T
    partial_value = lax.psum(product(weight, current), ("tok", "head"))
    for step in range(STEPS):
        left = orthonormal(product(upper, partial_value))
        back = product(weight.T, product(upper.T, left))
        back_gram, mixed = lax.psum((product(back.T, back), product(weight, back)), ("tok", "head"))
        lower = jnp.linalg.cholesky(back_gram)
        current = right_solve(lower, back)
        partial_value = right_solve(lower, mixed)
    return ((current * math.sqrt(OUT))[None], partial_value[None])


def solution(mesh):
    return jax.shard_map(
        on_device,
        mesh=mesh,
        in_specs=(
            P(("groups", "col"), ("tok", "head"), None),
            P(None, None, ("tok", "head")),
            P(("tok", "head"), None),
            P("groups", None),
        ),
        out_specs=(P(("groups", "col"), ("tok", "head"), None), P(("groups", "col"), None, None)),
        check_vma=False,
    )
```

profile of v0, /device:TPU:0, one launch (start us, length us, event | category | flops | bytes accessed | tf_op | source)
XLA Modules:
  0.0 636.7 jit_solution(14278276028762487654)
XLA Ops:
  7.2 12.1 %copy.36 = bf16[2,512,4096]{1,2,0:T(8,128)(2,1)} copy(bf16[2,512,4096]{2,1,0:T(8,128)(2,1)} %param.10) | data formatting | bytes 16777216 | tf_op args[1]
  19.3 11.8 %copy.37 = bf16[2,512,16,256]{3,1,2,0:T(8,128)(2,1)} copy(bf16[2,512,16,256]{1,3,2,0:T(8,128)(2,1)} %bitcast.212) | data formatting | bytes 16777216 | tf_op jit(solution)/shard_map/reshape | solution.py:39
  31.2 6.2 gather_fusion
  37.5 6.5 %copy.38 = bf16[512,16,256]{0,2,1:T(8,128)(2,1)} copy(bf16[512,16,256]{2,0,1:T(8,128)(2,1)} %bitcast.214) | data formatting | bytes 8388608 | tf_op jit(solution)/shard_map/transpose | solution.py:41
  44.0 1.7 fusion.4
  46.5 2.1 fusion.78
  48.9 64.6 %all-reduce.13.cloned.1.call-done = (f32[512,256]{1,0:T(8,128)}, f32[512,512]{0,1:T(8,128)}) async-done(((f32[512,256]{1,0:T(8,128)}, f32[512,512]{0,1:T(8,128)}), (f32[512,256]{1,0:T(8,128)}, f32[512,512]{0,1:T(8,128)})) %all-reduce.13.cloned.1.call-update) | async-done | bytes 1572880 | tf_op jit(solution)/shard_map/psum | solution.py:46
  113.5 1.6 copy.40
  115.1 1.5 fusion.3
  116.6 11.7 %cholesky.136 = f32[128,128]{1,0:T(8,128)S(1)} custom-call(f32[128,128]{1,0:T(8,128)S(1)} %cholesky.531), custom_call_target="Cholesky" | custom-call | tf_op jit(solution)/shard_map/jit(cholesky)/cholesky | solution.py:45
  128.5 9.8 %custom-call.35 = f32[1,128,128]{1,2,0:T(8,128)S(1)} custom-call(f32[1,128,128]{2,1,0:T(8,128)S(1)} %get-tuple-element.120), custom_call_target="InvertDiagBlocksLowerTriangular" | custom-call | tf_op jit(solution)/shard_map/jit(cholesky)/cholesky | solution.py:45
  139.0 11.7 %cholesky.159 = f32[128,128]{1,0:T(8,128)S(1)} custom-call(f32[128,128]{1,0:T(8,128)S(1)} %cholesky.535), custom_call_target="Cholesky" | custom-call | tf_op jit(solution)/shard_map/jit(cholesky)/cholesky | solution.py:45
  150.8 10.2 %custom-call.36 = f32[1,128,128]{1,2,0:T(8,128)S(1)} custom-call(f32[1,128,128]{2,1,0:T(8,128)S(1)} %get-tuple-element.117), custom_call_target="InvertDiagBlocksLowerTriangular" | custom-call | tf_op jit(solution)/shard_map/jit(cholesky)/cholesky | solution.py:45
  161.6 11.7 %cholesky.294 = f32[128,128]{1,0:T(8,128)S(1)} custom-call(f32[128,128]{1,0:T(8,128)S(1)} %cholesky.540), custom_call_target="Cholesky" | custom-call | tf_op jit(solution)/shard_map/jit(cholesky)/cholesky | solution.py:45
  173.4 9.8 %custom-call.51 = f32[1,128,128]{1,2,0:T(8,128)S(1)} custom-call(f32[1,128,128]{2,1,0:T(8,128)S(1)} %get-tuple-element.114), custom_call_target="InvertDiagBlocksLowerTriangular" | custom-call | tf_op jit(solution)/shard_map/jit(cholesky)/cholesky/custom-call.8 | solution.py:45
  183.8 11.7 %cholesky.307 = f32[128,128]{1,0:T(8,128)S(1)} custom-call(f32[128,128]{1,0:T(8,128)S(1)} %convolution_subtract_fusion.11), custom_call_target="Cholesky" | custom-call | tf_op jit(solution)/shard_map/jit(cholesky)/cholesky | solution.py:45
  200.0 1.4 fusion.18
  201.4 1.0 fusion.79
  202.6 11.7 %cholesky.427 = f32[128,128]{1,0:T(8,128)S(1)} custom-call(f32[128,128]{1,0:T(8,128)S(1)} %cholesky.544), custom_call_target="Cholesky" | custom-call | tf_op jit(solution)/shard_map/jit(cholesky)/cholesky | solution.py:22
  214.4 9.8 %custom-call.52 = f32[1,128,128]{1,2,0:T(8,128)S(1)} custom-call(f32[1,128,128]{2,1,0:T(8,128)S(1)} %get-tuple-element.110), custom_call_target="InvertDiagBlocksLowerTriangular" | custom-call | tf_op jit(solution)/shard_map/jit(cholesky)/cholesky/custom-call.8 | solution.py:22
  224.7 11.9 %cholesky.437 = f32[128,128]{1,0:T(8,128)S(1)} custom-call(f32[128,128]{1,0:T(8,128)S(1)} %convolution_subtract_fusion.10), custom_call_target="Cholesky" | custom-call | tf_op jit(solution)/shard_map/jit(cholesky)/cholesky | solution.py:22
  239.3 4.0 while.10
  239.9 1.4 bitcast_dynamic-update-slice_fusion.9
  241.9 1.4 bitcast_dynamic-update-slice_fusion.9
  243.3 19.7 %custom-call.53 = f32[2,128,128]{1,2,0:T(8,128)S(1)} custom-call(f32[2,128,128]{2,1,0:T(8,128)S(1)} %get-tuple-element.39), custom_call_target="InvertDiagBlocksLowerTriangular" | custom-call | tf_op jit(solution)/shard_map/triangular_solve/custom-call.9 | solution.py:18
  264.5 1.0 fusion.6
  265.5 6.2 fusion.80
  271.7 5.8 fusion.82
  277.5 7.8 %fusion.81 = f32[256,256]{0,1:T(8,128)} fusion(f32[4096,256]{1,0:T(8,128)S(1)} %fusion.80), kind=kOutput, calls=%fused_computation.178 | convolution fusion | flops 3221225472 | bytes 4456448 | tf_op jit(solution)/shard_map/dot_general | solution.py:14
  285.5 56.5 %all-reduce.11.cloned.1.call-done = (f32[512,256]{1,0:T(8,128)}, f32[256,256]{0,1:T(8,128)}) async-done(((f32[512,256]{1,0:T(8,128)}, f32[256,256]{0,1:T(8,128)}), (f32[512,256]{1,0:T(8,128)}, f32[256,256]{0,1:T(8,128)})) %all-reduce.11.cloned.1.call-update) | async-done | bytes 786448 | tf_op jit(solution)/shard_map/psum | solution.py:50
  342.0 1.1 copy.45
  344.1 11.7 %cholesky.454 = f32[128,128]{1,0:T(8,128)S(1)} custom-call(f32[128,128]{1,0:T(8,128)S(1)} %cholesky.547), custom_call_target="Cholesky" | custom-call | tf_op jit(solution)/shard_map/jit(cholesky)/cholesky | solution.py:51
  355.9 9.8 %custom-call.54 = f32[1,128,128]{1,2,0:T(8,128)S(1)} custom-call(f32[1,128,128]{2,1,0:T(8,128)S(1)} %get-tuple-element.106), custom_call_target="InvertDiagBlocksLowerTriangular" | custom-call | tf_op jit(solution)/shard_map/jit(cholesky)/cholesky/custom-call.8 | solution.py:51
  366.2 11.7 %cholesky.464 = f32[128,128]{1,0:T(8,128)S(1)} custom-call(f32[128,128]{1,0:T(8,128)S(1)} %convolution_subtract_fusion.9), custom_call_target="Cholesky" | custom-call | tf_op jit(solution)/shard_map/jit(cholesky)/cholesky | solution.py:51
  380.6 4.0 while.11
  381.2 1.4 bitcast_dynamic-update-slice_fusion.10
  383.2 1.4 bitcast_dynamic-update-slice_fusion.10
  384.6 19.9 %custom-call.55 = f32[2,128,128]{1,2,0:T(8,128)S(1)} custom-call(f32[2,128,128]{2,1,0:T(8,128)S(1)} %get-tuple-element.40), custom_call_target="InvertDiagBlocksLowerTriangular" | custom-call | tf_op jit(solution)/shard_map/triangular_solve/custom-call.9 | solution.py:18
  405.9 1.2 fusion.10
  408.4 11.7 %cholesky.481 = f32[128,128]{1,0:T(8,128)S(1)} custom-call(f32[128,128]{1,0:T(8,128)S(1)} %cholesky.550), custom_call_target="Cholesky" | custom-call | tf_op jit(solution)/shard_map/jit(cholesky)/cholesky | solution.py:22
  420.2 9.8 %custom-call.56 = f32[1,128,128]{1,2,0:T(8,128)S(1)} custom-call(f32[1,128,128]{2,1,0:T(8,128)S(1)} %get-tuple-element.102), custom_call_target="InvertDiagBlocksLowerTriangular" | custom-call | tf_op jit(solution)/shard_map/jit(cholesky)/cholesky/custom-call.8 | solution.py:22
  430.5 12.1 %cholesky.491 = f32[128,128]{1,0:T(8,128)S(1)} custom-call(f32[128,128]{1,0:T(8,128)S(1)} %convolution_subtract_fusion.8), custom_call_target="Cholesky" | custom-call | tf_op jit(solution)/shard_map/jit(cholesky)/cholesky | solution.py:22
  445.2 4.0 while.12
  445.8 1.4 bitcast_dynamic-update-slice_fusion.11
  447.8 1.4 bitcast_dynamic-update-slice_fusion.11
  449.2 19.7 %custom-call.57 = f32[2,128,128]{1,2,0:T(8,128)S(1)} custom-call(f32[2,128,128]{2,1,0:T(8,128)S(1)} %get-tuple-element.41), custom_call_target="InvertDiagBlocksLowerTriangular" | custom-call | tf_op jit(solution)/shard_map/triangular_solve/custom-call.9 | solution.py:18
  470.4 1.0 fusion.14
  471.4 5.7 fusion.84
  477.1 7.8 %fusion.85 = f32[256,256]{0,1:T(8,128)} fusion(f32[4096,256]{1,0:T(8,128)S(1)} %fusion.84), kind=kOutput, calls=%fused_computation.182 | convolution fusion | flops 3221225472 | bytes 4456448 | tf_op jit(solution)/shard_map/dot_general | solution.py:14
  484.9 5.8 fusion.86
  490.7 56.8 %all-reduce.9.cloned.1.call-done = (f32[256,256]{0,1:T(8,128)}, f32[512,256]{1,0:T(8,128)}) async-done(((f32[256,256]{0,1:T(8,128)}, f32[512,256]{1,0:T(8,128)}), (f32[256,256]{0,1:T(8,128)}, f32[512,256]{1,0:T(8,128)})) %all-reduce.9.cloned.1.call-update) | async-done | bytes 786448 | tf_op jit(solution)/shard_map/psum | solution.py:50
  547.5 1.1 copy.50
  549.6 11.9 %cholesky.508 = f32[128,128]{1,0:T(8,128)S(1)} custom-call(f32[128,128]{1,0:T(8,128)S(1)} %cholesky.553), custom_call_target="Cholesky" | custom-call | tf_op jit(solution)/shard_map/jit(cholesky)/cholesky | solution.py:51
  561.5 9.8 %custom-call.58 = f32[1,128,128]{1,2,0:T(8,128)S(1)} custom-call(f32[1,128,128]{2,1,0:T(8,128)S(1)} %get-tuple-element.98), custom_call_target="InvertDiagBlocksLowerTriangular" | custom-call | tf_op jit(solution)/shard_map/jit(cholesky)/cholesky/custom-call.8 | solution.py:51
  571.8 11.7 %cholesky.518 = f32[128,128]{1,0:T(8,128)S(1)} custom-call(f32[128,128]{1,0:T(8,128)S(1)} %convolution_subtract_fusion.7), custom_call_target="Cholesky" | custom-call | tf_op jit(solution)/shard_map/jit(cholesky)/cholesky | solution.py:51
  586.1 3.8 while.9
  586.7 1.3 bitcast_dynamic-update-slice_fusion.8
  588.6 1.3 bitcast_dynamic-update-slice_fusion.8
  589.9 19.9 %custom-call.37 = f32[2,128,128]{1,2,0:T(8,128)S(1)} custom-call(f32[2,128,128]{2,1,0:T(8,128)S(1)} %get-tuple-element.20), custom_call_target="InvertDiagBlocksLowerTriangular" | custom-call | tf_op jit(solution)/shard_map/triangular_solve | solution.py:18
  609.8 3.7 fusion
  613.6 3.6 convolution_subtract_fusion
  617.1 2.0 convolution_bitcast_fusion
  619.2 2.4 maximum_multiply_fusion
  621.6 5.7 copy.52
  (127 shorter events, 28.0 us)
Async XLA Ops:
  7.2 38.5 %copy-start = (bf16[4096,256]{1,0:T(8,128)(2,1)S(1)}, bf16[4096,256]{1,0:T(8,128)(2,1)}, u32[]{:S(2)}) copy-start(bf16[4096,256]{1,0:T(8,128)(2,1)} %param.11) | copy-start | bytes 6291460
  7.2 106.4 %all-reduce.13.cloned.1.call-start = ((), (), s32[]{:S(2)}) async-start(), calls=%async_computation.2 | async-start | bytes 3145728 | tf_op jit(solution)/shard_map/psum | solution.py:46
  19.3 11.8 %copy-start.10 = (s32[2,128]{1,0:T(2,128)S(1)}, s32[2,128]{1,0:T(2,128)}, u32[]{:S(2)}) copy-start(s32[2,128]{1,0:T(2,128)} %param.12) | copy-start | bytes 3076
  37.5 6.5 %copy-start.11 = (bf16[1,1024,512]{2,1,0:T(8,128)(2,1)S(1)}, bf16[1,1024,512]{2,1,0:T(8,128)(2,1)}, u32[]{:S(2)}) copy-start(bf16[1,1024,512]{2,1,0:T(8,128)(2,1)} %param.9) | copy-start | bytes 3145732
  44.0 2.6 copy-start.2
  48.6 293.4 %all-reduce.11.cloned.1.call-start = ((), (), s32[]{:S(2)}) async-start(), calls=%async_computation.1 | async-start | bytes 1572864 | tf_op jit(solution)/shard_map/psum | solution.py:50
  115.1 84.9 %copy-start.7 = (f32[512,256]{1,0:T(8,128)S(1)}, f32[512,256]{1,0:T(8,128)}, u32[]{:S(2)}) copy-start(f32[512,256]{1,0:T(8,128)} %get-tuple-element.85) | copy-start | bytes 1572868
  265.5 6.2 copy-start.3
  285.3 262.2 %all-reduce.9.cloned.1.call-start = ((), (), s32[]{:S(2)}) async-start(), calls=%async_computation | async-start | bytes 1572864 | tf_op jit(solution)/shard_map/psum | solution.py:50
  342.0 62.5 %copy-start.9 = (f32[512,256]{1,0:T(8,128)S(1)}, f32[512,256]{1,0:T(8,128)}, u32[]{:S(2)}) copy-start(f32[512,256]{1,0:T(8,128)} %get-tuple-element.83) | copy-start | bytes 1572868
  477.1 7.8 %copy-start.5 = (f32[4096,256]{1,0:T(8,128)}, f32[4096,256]{1,0:T(8,128)S(1)}, u32[]{:S(2)}) copy-start(f32[4096,256]{1,0:T(8,128)S(1)} %fusion.84) | copy-start | bytes 12582916
  477.1 7.8 %copy-start.4 = (bf16[512,16,256]{0,2,1:T(8,128)(2,1)S(1)}, bf16[512,16,256]{0,2,1:T(8,128)(2,1)}, u32[]{:S(2)}) copy-start(bf16[512,16,256]{0,2,1:T(8,128)(2,1)} %copy.38) | copy-start | bytes 12582916
  609.8 3.8 copy-start.6
  619.2 10.6 %copy-start.1 = (bf16[4096,256]{1,0:T(8,128)(2,1)S(1)}, bf16[4096,256]{1,0:T(8,128)(2,1)}, u32[]{:S(2)}) copy-start(bf16[4096,256]{1,0:T(8,128)(2,1)} %param.11) | copy-start | bytes 6291460
  621.6 5.7 copy-start.8
Sparse Core Ops, SparseCore 0:
  48.8 64.7 all-reduce.12
  285.4 56.5 all-reduce.10
  490.8 56.5 all-reduce.8
where the time goes:
time: 641 us; the launch traced here: 637 us
  other arithmetic  303 us (47%)
  waiting for transfers between devices  178 us (28%)
  matrix products  68.2 us (11%)
  local copies, waits for them, and re-layouts  64.2 us (10%)
  between operations  22.5 us (4%)
    psum x2, waiting for transfers between devices, on_device(): lax.psum((product(back.T, back), product(weight, back)), ('tok', 'head'))  113 us
    another operation x9, other arithmetic, right_solve(): lax.linalg.triangular_solve(lower, block, left_side=False, lower=True, tr...  79.3 us
    another operation x14, other arithmetic, on_device(): upper = jnp.linalg.cholesky(incoming).T  78.7 us
    another operation x14, other arithmetic, orthonormal(): lower = jnp.linalg.cholesky(product(block.T, block))  69.7 us
    another operation x14, other arithmetic, on_device(): lower = jnp.linalg.cholesky(back_gram)  69.3 us
    psum x1, waiting for transfers between devices, on_device(): partial_value = lax.psum(product(weight, current), ('tok', 'head'))  64.6 us
    dot_general x13, matrix products, product(): return jnp.dot(left, right, precision=lax.Precision.HIGHEST)  47.8 us
    unnamed x27, local copies, waits for them, and re-layouts  19.6 us
  transfers between devices with their start and end apart: 3, of which 3 were waited for; matrix products, arithmetic and copies ran while one was open for 0% of the time, Pallas kernels for 0%

commit v1 on v0

v1 whole, which is shorter than its diff:
```python
import math

import jax
import jax.numpy as jnp
from jax import lax
from jax.sharding import PartitionSpec as P

OUT = 32768
STEPS = 2
HEAD_OUT = 256


def product(left, right):
    return jnp.dot(left, right, precision=lax.Precision.HIGHEST)


def chosen_weight(weights, layer_pick):
    stack_count, _, col_count = weights.shape
    heads_here = col_count // HEAD_OUT
    slot = lax.axis_index("col")
    first_head = lax.axis_index(("tok", "head")) * heads_here
    picks = lax.dynamic_slice_in_dim(layer_pick[slot], first_head, heads_here, 0)
    pick_of_col = jnp.repeat(picks, HEAD_OUT)[None]
    weight = weights[0]
    for layer in range(1, stack_count):
        weight = jnp.where(pick_of_col == layer, weights[layer], weight)
    return weight


def orthonormal_coefficients(back, weight_gram):
    back_gram = product(back.T, product(weight_gram, back))
    lower = jnp.linalg.cholesky(back_gram)
    return lax.linalg.triangular_solve(lower, back, left_side=False, lower=True, transpose_a=True)


def on_device(latents, weights, start_basis, layer_pick):
    act = latents[0]
    weight = chosen_weight(weights, layer_pick)
    gram = jnp.dot(act.T, act, preferred_element_type=jnp.float32)
    weight_gram = jnp.dot(weight, weight.T, preferred_element_type=jnp.float32)
    image = jnp.dot(weight, start_basis, preferred_element_type=jnp.float32)
    gram, weight_gram, image = lax.psum((gram, weight_gram, image), ("tok", "head"))
    gram = gram / jnp.mean(jnp.diag(gram))
    image = image / jnp.sqrt(jnp.mean(image * image))
    for step in range(STEPS):
        coefficients = orthonormal_coefficients(product(gram, image), weight_gram)
        image = product(weight_gram, coefficients)
    scaled = coefficients * math.sqrt(OUT)
    high = lax.reduce_precision(scaled, 8, 7)
    low = scaled - high
    pieces = jnp.concatenate([high.astype(jnp.bfloat16), low.astype(jnp.bfloat16)], 1)
    both = jnp.dot(weight.T, pieces, preferred_element_type=jnp.float32)
    rank = scaled.shape[1]
    return ((both[:, :rank] + both[:, rank:])[None], image[None])


def solution(mesh):
    return jax.shard_map(
        on_device,
        mesh=mesh,
        in_specs=(
            P(("groups", "col"), ("tok", "head"), None),
            P(None, None, ("tok", "head")),
            P(("tok", "head"), None),
            P("groups", None),
        ),
        out_specs=(P(("groups", "col"), ("tok", "head"), None), P(("groups", "col"), None, None)),
        check_vma=False,
    )
```

time: 641 us -> 279 us (0.44)
  other arithmetic: 303 us -> 120 us
  waiting for transfers between devices: 178 us -> 72.6 us
  local copies, waits for them, and re-layouts: 64.2 us -> 21.4 us
  matrix products: 68.2 us -> 41.5 us
    another operation x51 -> x18, other arithmetic: 297 us -> 112 us  [the longest x13 69.2 us: orthonormal_coefficients(): lower = jnp.linalg.cholesky(back_gram)]
    psum x3 -> x1, waiting for transfers between devices: 178 us -> 72.6 us  [on_device(): lax.psum((gram, weight_gram, image), ('tok', 'head'))]
    dot_general x13 -> x8, matrix products: 47.8 us -> 11.4 us  [product(): return jnp.dot(left, right, precision=lax.Precision.HIGHEST)]
    dot_general x1 -> x4, matrix products: 1.73 us -> 19.1 us  [the longest x1 9.33 us: on_device(): weight_gram = jnp.dot(weight, weight.T, preferred_element_type=jnp.float32)]
    unnamed x27 -> x24, local copies, waits for them, and re-layouts: 19.6 us -> 2.74 us
    reshape x1 -> x0, local copies, waits for them, and re-layouts: 11.8 us -> none  [on_device(): stacked = weights.reshape(stack_count, width, heads_here, HEAD_OUT)]
    another operation x29 -> x10, matrix products: 18.7 us -> 11 us  [the longest x6 6.66 us: orthonormal_coefficients(): lax.linalg.triangular_solve(lower, back, left_side=False, lower=True, tra...]
    another operation x41 -> x19, local copies, waits for them, and re-layouts: 16 us -> 8.25 us  [the longest x15 8.2 us: orthonormal_coefficients(): lax.linalg.triangular_solve(lower, back, left_side=False, lower=True, tra...]
  transfers between devices with their start and end apart: 3 -> 1, of which waited for: 3 -> 1; matrix products, arithmetic and copies ran while one was open for 0% -> 0% of each run, Pallas kernels for 0% -> 0%
where the time goes in v1:
time: 279 us; the launch traced here: 274 us
  other arithmetic  120 us (43%)
  waiting for transfers between devices  72.6 us (26%)
  matrix products  41.5 us (15%)
  local copies, waits for them, and re-layouts  21.4 us (8%)
  between operations  18.4 us (7%)
    psum x1, waiting for transfers between devices, on_device(): lax.psum((gram, weight_gram, image), ('tok', 'head'))  72.6 us
    another operation x13, other arithmetic, orthonormal_coefficients(): lower = jnp.linalg.cholesky(back_gram)  69.2 us
    another operation x5, other arithmetic, orthonormal_coefficients(): lax.linalg.triangular_solve(lower, back, left_side=False, lower=True, tra...  42.9 us
    dot_general x8, matrix products, product(): return jnp.dot(left, right, precision=lax.Precision.HIGHEST)  11.4 us
    dot_general x1, matrix products, on_device(): weight_gram = jnp.dot(weight, weight.T, preferred_element_type=jnp.float32)  9.33 us
    gather x1, local copies, waits for them, and re-layouts, on_device(): gram = gram / jnp.mean(jnp.diag(gram))  8.61 us
    another operation x15, local copies, waits for them, and re-layouts, orthonormal_coefficients(): lax.linalg.triangular_solve(lower, back, left_side=False, lower=True, tra...  8.2 us
    another operation x6, matrix products, orthonormal_coefficients(): lax.linalg.triangular_solve(lower, back, left_side=False, lower=True, tra...  6.66 us
  transfers between devices with their start and end apart: 1, of which 1 were waited for; matrix products, arithmetic and copies ran while one was open for 0% of the time, Pallas kernels for 0%

profile of v1, /device:TPU:0, one launch (start us, length us, event | category | flops | bytes accessed | tf_op | source)
XLA Modules:
  0.0 274.1 jit_solution(14214524154709775036)
XLA Ops:
  7.2 0.0 all-reduce.4.cloned.1.call-start
  7.2 0.9 compare_bitcast_fusion
  8.1 0.1 broadcast_in_dim.26
  8.2 9.3 %fusion.1 = f32[512,512]{1,0:T(8,128)} fusion(pred[4096]{0:T(1024)(128)(4,1)S(1)} %eq.21, bf16[2,512,4096]{2,1,0:T(8,128)(2,1)} %param.8), kind=kOutput, calls=%fused_computation.7 | convolution fusion | flops 2149580800 | bytes 9441280 | tf_op jit(solution)/shard_map/dot_general | solution.py:40
  17.6 2.1 fusion.10
  19.6 1.7 fusion.7
  21.4 0.0 all-reduce.4.cloned.1.call-update
  21.4 72.6 %all-reduce.4.cloned.1.call-done = (f32[512,512]{1,0:T(8,128)}, f32[512,256]{1,0:T(8,128)}, f32[512,512]{1,0:T(8,128)}) async-done(((f32[512,512]{1,0:T(8,128)}, f32[512,256]{1,0:T(8,128)}, f32[512,512]{1,0:T(8,128)}), (f32[512,512]{1,0:T(8,128)}, f32[512,256]{1,0:T(8,128)}, f32[512,512]{1,0:T(8,128)})) %all-reduce.4.cloned.1.call-update) | async-done | bytes 2621456 | tf_op jit(solution)/shard_map/psum | solution.py:42
  94.0 1.9 multiply_reduce_fusion
  96.5 8.6 %gather_fusion = f32[512]{0:T(512)S(1)} fusion(f32[512,512]{1,0:T(8,128)} %get-tuple-element.38, s32[512]{0:T(512)S(1)} %bitcast.97), kind=kCustom, calls=%fused_computation | custom fusion | bytes 8192 | tf_op jit(solution)/shard_map/jit(_diag)/jit(diagonal)/cond/branch_0_fun/gather | solution.py:43
  105.2 0.6 reduce_sum.18
  106.4 2.4 fusion.19
  108.8 1.0 fusion.48
  109.8 1.0 fusion.49
  110.8 0.8 copy.8
  111.7 1.0 fusion.27
  112.7 0.7 copy-done.7
  113.4 11.7 %cholesky.130 = f32[128,128]{1,0:T(8,128)S(1)} custom-call(f32[128,128]{1,0:T(8,128)S(1)} %cholesky.194), custom_call_target="Cholesky" | custom-call | tf_op jit(solution)/shard_map/jit(cholesky)/cholesky | solution.py:32
  125.1 9.8 %custom-call.15 = f32[1,128,128]{1,2,0:T(8,128)S(1)} custom-call(f32[1,128,128]{2,1,0:T(8,128)S(1)} %get-tuple-element.52), custom_call_target="InvertDiagBlocksLowerTriangular" | custom-call | tf_op jit(solution)/shard_map/jit(cholesky)/cholesky | solution.py:32
  135.0 1.0 constant_dynamic-update-slice_fusion.3
  136.0 1.1 convolution_subtract_fusion.3
  137.1 12.1 %cholesky.147 = f32[128,128]{1,0:T(8,128)S(1)} custom-call(f32[128,128]{1,0:T(8,128)S(1)} %convolution_subtract_fusion.3), custom_call_target="Cholesky" | custom-call | tf_op jit(solution)/shard_map/jit(cholesky)/cholesky | solution.py:32
  149.2 0.7 compare_reduce_fusion.2
  151.2 1.0 select_select_fusion.1
  152.2 0.1 broadcast.128
  152.3 4.1 %while.4 = (s32[]{:T(128)}, f32[256,256]{1,0:T(8,128)S(1)}, s32[2,2]{1,0:T(2,128)S(1)}, f32[2,128,128]{2,1,0:T(8,128)S(1)}, s32[]{:T(128)}) while((s32[]{:T(128)}, f32[256,256]{1,0:T(8,128)S(1)}, s32[2,2]{1,0:T(2,128)S(1)}, f32[2,128,128]{2,1,0:T(8,128)S(1)}, s32[]{:T(128)}) %tuple.48), condition=%wide.while_cond, body=%wide.while_body.sunk | while | flops 2 | bytes 131189 | solution.py:33
  152.3 0.6 fusion.74
  152.9 1.4 bitcast_dynamic-update-slice_fusion.4
  154.4 0.6 fusion.74
  155.0 1.4 bitcast_dynamic-update-slice_fusion.4
  156.4 0.6 copy-done.9
  157.1 20.5 %custom-call.16 = f32[2,128,128]{1,2,0:T(8,128)S(1)} custom-call(f32[2,128,128]{2,1,0:T(8,128)} %copy-done.9), custom_call_target="InvertDiagBlocksLowerTriangular" | custom-call | tf_op jit(solution)/shard_map/triangular_solve/custom-call.0 | solution.py:33
  177.6 1.4 fusion.24
  178.9 1.5 convolution_subtract_fusion.1
  180.5 0.4 fusion.33
  180.9 1.0 fusion.12
  181.9 2.2 fusion.21
  184.2 1.0 fusion.50
  185.2 1.0 fusion.51
  186.2 0.8 copy.9
  187.0 1.0 fusion.26
  188.0 0.7 copy-done.6
  188.7 11.7 %cholesky.164 = f32[128,128]{1,0:T(8,128)S(1)} custom-call(f32[128,128]{1,0:T(8,128)S(1)} %cholesky.197), custom_call_target="Cholesky" | custom-call | tf_op jit(solution)/shard_map/jit(cholesky)/cholesky | solution.py:32
  200.5 0.7 compare_reduce_fusion.1
  201.2 9.8 %custom-call.17 = f32[1,128,128]{1,2,0:T(8,128)S(1)} custom-call(f32[1,128,128]{2,1,0:T(8,128)S(1)} %get-tuple-element.48), custom_call_target="InvertDiagBlocksLowerTriangular" | custom-call | tf_op jit(solution)/shard_map/jit(cholesky)/cholesky | solution.py:32
  211.1 1.0 constant_dynamic-update-slice_fusion.1
  212.1 1.1 convolution_subtract_fusion.2
  213.2 11.9 %cholesky.181 = f32[128,128]{1,0:T(8,128)S(1)} custom-call(f32[128,128]{1,0:T(8,128)S(1)} %convolution_subtract_fusion.2), custom_call_target="Cholesky" | custom-call | tf_op jit(solution)/shard_map/jit(cholesky)/cholesky | solution.py:32
  225.1 0.6 compare_reduce_fusion
  227.0 1.0 select_select_fusion
  228.0 4.1 %while.5 = (s32[]{:T(128)}, f32[256,256]{1,0:T(8,128)S(1)}, s32[2,2]{1,0:T(2,128)S(1)}, f32[2,128,128]{2,1,0:T(8,128)S(1)}, s32[]{:T(128)}) while((s32[]{:T(128)}, f32[256,256]{1,0:T(8,128)S(1)}, s32[2,2]{1,0:T(2,128)S(1)}, f32[2,128,128]{2,1,0:T(8,128)S(1)}, s32[]{:T(128)}) %tuple.57), condition=%wide.while_cond.clone, body=%wide.while_body.clone.sunk | while | flops 2 | bytes 131189 | solution.py:33
  228.1 0.6 fusion.75
  228.6 1.4 bitcast_dynamic-update-slice_fusion.5
  230.1 0.6 fusion.75
  230.7 1.4 bitcast_dynamic-update-slice_fusion.5
  232.2 0.6 copy-done.8
  232.8 20.5 %custom-call.18 = f32[2,128,128]{1,2,0:T(8,128)S(1)} custom-call(f32[2,128,128]{2,1,0:T(8,128)} %copy-done.8), custom_call_target="InvertDiagBlocksLowerTriangular" | custom-call | tf_op jit(solution)/shard_map/triangular_solve/custom-call.0 | solution.py:33
  253.3 1.4 fusion.22
  254.7 1.5 convolution_subtract_fusion
  256.2 0.4 fusion.29
  256.6 1.8 convolution_bitcast_fusion
  258.5 0.1 reduce-precision_convert_fusion
  258.6 6.0 %fusion.9 = f32[4096,512]{1,0:T(8,128)S(1)} fusion(pred[4096]{0:T(1024)(128)(4,1)S(1)} %eq.21, bf16[2,512,4096]{2,1,0:T(8,128)(2,1)} %param.8, bf16[512,256]{0,1:T(8,128)(2,1)S(1)} %get-tuple-element.44, bf16[512,256]{0,1:T(8,128)(2,1)S(1)} %get-tuple-element.43), kind=kOutput, calls=%fused_computation.23 | convolution fusion | flops 2150629376 | bytes 17305600 | tf_op jit(solution)/shard_map/dot_general | solution.py:52
  264.5 2.5 fusion
  (37 shorter events, 0.3 us)
Async XLA Ops:
  7.2 10.4 %copy-start = (bf16[4096,256]{1,0:T(8,128)(2,1)S(1)}, bf16[4096,256]{1,0:T(8,128)(2,1)}, u32[]{:S(2)}) copy-start(bf16[4096,256]{1,0:T(8,128)(2,1)} %param.9) | copy-start | bytes 6291460
  7.2 86.8 %all-reduce.4.cloned.1.call-start = ((), (), s32[]{:S(2)}) async-start(), calls=%async_computation | async-start | bytes 5242880 | tf_op jit(solution)/shard_map/psum | solution.py:42
  8.2 9.3 %copy-start.10 = (bf16[2,512,4096]{2,1,0:T(8,128)(2,1)S(1)}, bf16[2,512,4096]{2,1,0:T(8,128)(2,1)}, u32[]{:S(2)}) copy-start(bf16[2,512,4096]{2,1,0:T(8,128)(2,1)} %param.8) | copy-start | bytes 25165828
  17.6 2.1 copy-start.11
  94.0 14.8 %copy-start.1 = (f32[512,512]{1,0:T(8,128)S(1)}, f32[512,512]{1,0:T(8,128)}, u32[]{:S(2)}) copy-start(f32[512,512]{1,0:T(8,128)} %get-tuple-element.36) | copy-start | bytes 3145732
  108.8 1.0 copy-start.2
  112.7 0.7 copy-start.7
  149.2 2.0 copy-start.4
  156.4 0.7 copy-start.9
  184.2 1.0 copy-start.3
  188.0 0.7 copy-start.6
  225.1 1.9 copy-start.5
  232.1 0.7 copy-start.8
Sparse Core Ops, SparseCore 0:
  21.5 72.4 all-reduce.3

commit v2 on v0

v2 whole, which is shorter than its diff:
```python
import functools
import math

import jax
import jax.numpy as jnp
from jax import lax
from jax.experimental import pallas as pl
from jax.experimental.pallas import tpu as pltpu
from jax.sharding import PartitionSpec as P

OUT = 32768
STEPS = 2
HEAD_OUT = 256
HALF = 256
PANEL = 8
BLOCK = 128
MESH = pl.DeviceIdType.MESH


def pack(packed, gram, first, diagonal):
    row = lax.broadcasted_iota(jnp.int32, (HALF, HALF), 0)
    column = lax.broadcasted_iota(jnp.int32, (HALF, HALF), 1)
    packed[first:first + HALF, :] = gram[:HALF, HALF:]
    bottom = gram[HALF:, HALF:]
    packed[first + HALF:first + 2 * HALF, :] = jnp.where(row >= column, gram[:HALF, :HALF], bottom)
    packed[diagonal:diagonal + 1, :] = jnp.sum(jnp.where(row == column, bottom, 0.0), axis=0, keepdims=True)


def local_sums_kernel(together, picks, act, start, *refs):
    weights, (packed, gram, weight_gram) = refs[:together], refs[together:]
    at = pl.program_id(0)
    width = gram.shape[0]

    @pl.when(at == 0)
    def _():
        packed[...] = jnp.zeros_like(packed)
        gram[...] = jnp.zeros_like(gram)
        weight_gram[...] = jnp.zeros_like(weight_gram)

    weight = jnp.concatenate([w[0] for w in weights], axis=1)
    gram[...] += lax.dot_general(act[...], act[...], (((0,), (0,)), ((), ())), preferred_element_type=jnp.float32)
    weight_gram[...] += lax.dot_general(weight, weight, (((1,), (1,)), ((), ())), preferred_element_type=jnp.float32)
    packed[:width, :] += jnp.dot(weight, start[...], preferred_element_type=jnp.float32)

    @pl.when(at == pl.num_programs(0) - 1)
    def _():
        pack(packed, gram, width, width + 4 * HALF)
        pack(packed, weight_gram, width + 2 * HALF, width + 4 * HALF + 1)


def weight_specs(together, width):
    def spec(k):
        return pl.BlockSpec((1, width, HEAD_OUT), lambda at, picks: (picks[at * together + k], 0, at * together + k))

    return [spec(k) for k in range(together)]


def local_sums(picks, act, start, weights, rows):
    width = act.shape[1]
    rank = start.shape[1]
    heads_here = picks.shape[0]
    together = math.gcd(heads_here, 4)
    steps = heads_here // together
    return pl.pallas_call(
        functools.partial(local_sums_kernel, together),
        out_shape=jax.ShapeDtypeStruct((rows, rank), jnp.float32),
        grid_spec=pltpu.PrefetchScalarGridSpec(
            num_scalar_prefetch=1,
            grid=(steps,),
            in_specs=[
                pl.BlockSpec((act.shape[0] // steps, width), lambda at, picks: (at, 0)),
                pl.BlockSpec((start.shape[0] // steps, rank), lambda at, picks: (at, 0)),
            ] + weight_specs(together, width),
            out_specs=pl.BlockSpec((rows, rank), lambda at, picks: (0, 0)),
            scratch_shapes=[pltpu.VMEM((width, width), jnp.float32)] * 2,
        ),
        compiler_params=pltpu.CompilerParams(vmem_limit_bytes=48 * 2**20),
        name="local_sums",
    )(picks, act, start, *[weights] * together)


def sum_kernel(count, x, out, from_core, chip_sum, from_chips, sems):
    me = lax.axis_index("tok")
    core = lax.axis_index("head")
    half = x.shape[0] // 2
    shard = half // count
    mine = core * half
    theirs = (1 - core) * half
    partner = {"head": 1 - core}

    def remote(source, target, stage, slot, device):
        return pltpu.make_async_remote_copy(
            src_ref=source, dst_ref=target, send_sem=sems.at[stage, 0, slot], recv_sem=sems.at[stage, 1, slot],
            device_id=device, device_id_type=MESH)

    def rows_of(base, index):
        return pl.ds(pl.multiple_of(base + index * shard, 8), shard)

    peers = [lax.rem(me + d, count) for d in range(count)]
    barrier = pltpu.get_barrier_semaphore()
    pl.semaphore_signal(barrier, inc=1, device_id=partner, device_id_type=MESH)
    for d in range(1, count):
        pl.semaphore_signal(barrier, inc=1, device_id={"tok": peers[d]}, device_id_type=MESH)
    pl.semaphore_wait(barrier, count)

    order = list(range(1, count)) + [0]
    first = [remote(x.at[rows_of(theirs, peers[d])], from_core.at[d], 0, d, partner) for d in range(count)]
    for d in order:
        first[d].start()
    second = [None] + [remote(chip_sum.at[d], from_chips.at[d], 1, d, {"tok": peers[d]}) for d in range(1, count)]
    for d in order:
        first[d].wait_recv()
        chip_sum[d] = x[rows_of(mine, peers[d]), :] + from_core[d]
        if d:
            second[d].start()
    total = chip_sum[0]
    for d in range(1, count):
        second[d].wait_recv()
        total = total + from_chips[d]
    own = rows_of(mine, me)
    out[own, :] = total
    third = [remote(out.at[own], out.at[own], 2, d, {"tok": peers[d]} if d else partner) for d in range(count)]
    for d in order:
        third[d].start()
    fourth = [None]
    for d in range(1, count):
        third[d].wait_recv()
        source = out.at[rows_of(mine, lax.rem(me - d + count, count))]
        fourth.append(remote(source, source, 3, d, partner))
        fourth[d].start()
    third[0].wait_recv()
    for d in range(1, count):
        fourth[d].wait_recv()
    for d in range(count):
        first[d].wait_send()
        third[d].wait_send()
        if d:
            second[d].wait_send()
            fourth[d].wait_send()


def summed(x):
    count = lax.axis_size("tok")
    shard = x.shape[0] // 2 // count
    slots = pltpu.VMEM((count, shard, x.shape[1]), jnp.float32)
    return pl.pallas_call(
        functools.partial(sum_kernel, count),
        out_shape=jax.ShapeDtypeStruct(x.shape, jnp.float32),
        in_specs=[pl.BlockSpec(memory_space=pltpu.VMEM)],
        out_specs=pl.BlockSpec(memory_space=pltpu.VMEM),
        scratch_shapes=[slots, slots, slots, pltpu.SemaphoreType.DMA((4, 2, count))],
        compiler_params=pltpu.CompilerParams(collective_id=0, has_side_effects=True, vmem_limit_bytes=48 * 2**20),
        name="summed",
    )(x)


def exact_dot(left, right, contract=(1, 0)):
    dims = (((contract[0],), (contract[1],)), ((), ()))
    return lax.dot_general(left, right, dims, precision=lax.Precision.HIGHEST, preferred_element_type=jnp.float32)


def inverse_factor(work, size):
    sublane = lax.broadcasted_iota(jnp.int32, (PANEL, 2 * size), 0)
    for first in range(0, size, PANEL):
        rows = work[first:first + PANEL, :]
        columns = [jnp.broadcast_to(rows[:, first + c:first + c + 1], (PANEL, 128)) for c in range(PANEL)]
        scale = jnp.zeros((PANEL, 128), jnp.float32)
        for c in range(PANEL):
            pivot = jnp.broadcast_to(columns[c][c:c + 1, :], (PANEL, 128))
            scale = jnp.where(sublane[:, :128] == c, pivot, scale)
            if c == PANEL - 1:
                break
            factor = jnp.where(sublane[:, :128] > c, columns[c] / pivot, 0.0)
            for later in range(c + 1, PANEL):
                columns[later] = columns[later] - factor * columns[later][c:c + 1, :]
            wide = jnp.concatenate([factor] * (2 * size // 128), axis=1)
            rows = rows - wide * rows[c:c + 1, :]
        inverse_root = lax.rsqrt(scale)
        rows = rows * jnp.concatenate([inverse_root] * (2 * size // 128), axis=1)
        work[first:first + PANEL, :] = rows
        rest = first + PANEL
        if rest < size:
            update = exact_dot(rows[:, :size], rows, (0, 0))
            work[rest:, :] = work[rest:, :] - update[rest:, :]
    return work[:, size:]


def unpacked(packed, first, diagonal):
    corner = packed[first:first + HALF, :]
    triangles = packed[first + HALF:first + 2 * HALF, :]
    row = lax.broadcasted_iota(jnp.int32, (HALF, HALF), 0)
    column = lax.broadcasted_iota(jnp.int32, (HALF, HALF), 1)
    flipped = triangles.T
    top = jnp.where(row >= column, triangles, flipped)
    bottom = jnp.where(row < column, triangles, flipped)
    bottom = jnp.where(row == column, jnp.broadcast_to(packed[diagonal:diagonal + 1, :], (HALF, HALF)), bottom)
    return jnp.concatenate([
        jnp.concatenate([top, corner], axis=1),
        jnp.concatenate([corner.T, bottom], axis=1),
    ], axis=0)


def chain_kernel(packed, image_out, pieces_out, weight_gram_ref, image_work, back_work, work):
    width, rank = image_work.shape
    row = lax.broadcasted_iota(jnp.int32, (width, width), 0)
    column = lax.broadcasted_iota(jnp.int32, (width, width), 1)
    gram = unpacked(packed, width, width + 4 * HALF)
    gram = gram / (jnp.sum(jnp.where(row == column, gram, 0.0)) / width)
    weight_gram_ref[...] = unpacked(packed, width + 2 * HALF, width + 4 * HALF + 1)
    image = packed[:width, :]
    image_work[...] = image / jnp.sqrt(jnp.mean(image * image))
    eye = (row[:BLOCK, :BLOCK] == column[:BLOCK, :BLOCK]).astype(jnp.float32)

    def step(_, carry):
        back = exact_dot(gram, image_work[...])
        mixed = exact_dot(weight_gram_ref[...], back)
        square = exact_dot(back, mixed, (0, 0))
        pieces = []
        count = rank // BLOCK
        schur = {}
        for i in range(count):
            for j in range(i + 1):
                schur[i, j] = square[i * BLOCK:(i + 1) * BLOCK, j * BLOCK:(j + 1) * BLOCK]
        inverse = []
        below = {}
        done = []
        for i in range(count):
            current = schur[i, i]
            work[:, :BLOCK] = current
            work[:, BLOCK:] = eye
            inv = inverse_factor(work, BLOCK)
            lower_mask = row[:BLOCK, :BLOCK] >= column[:BLOCK, :BLOCK]
            inv = jnp.where(lower_mask, inv, 0.0)
            part_back = back[:, i * BLOCK:(i + 1) * BLOCK]
            part_mixed = mixed[:, i * BLOCK:(i + 1) * BLOCK]
            for j in range(i):
                part_back = part_back - exact_dot(done[j][0], below[i, j], (1, 1))
                part_mixed = part_mixed - exact_dot(done[j][1], below[i, j], (1, 1))
            part_back = exact_dot(part_back, inv, (1, 1))
            part_mixed = exact_dot(part_mixed, inv, (1, 1))
            done.append((part_back, part_mixed))
            for k in range(i + 1, count):
                below[k, i] = exact_dot(schur[k, i], inv, (1, 1))
            for k in range(i + 1, count):
                for m in range(i + 1, k + 1):
                    schur[k, m] = schur[k, m] - exact_dot(below[k, i], below[m, i], (1, 1))
        back_work[...] = jnp.concatenate([d[0] for d in done], axis=1)
        image_work[...] = jnp.concatenate([d[1] for d in done], axis=1)
        return carry

    lax.fori_loop(0, STEPS, step, 0)
    image_out[...] = image_work[...]
    scaled = back_work[...] * math.sqrt(OUT)
    high = scaled.astype(jnp.bfloat16)
    pieces_out[:, :rank] = high
    pieces_out[:, rank:] = (scaled - high.astype(jnp.float32)).astype(jnp.bfloat16)


def chain(packed, width, rank):
    return pl.pallas_call(
        chain_kernel,
        out_shape=(jax.ShapeDtypeStruct((width, rank), jnp.float32), jax.ShapeDtypeStruct((width, 2 * rank), jnp.bfloat16)),
        in_specs=[pl.BlockSpec(memory_space=pltpu.VMEM)],
        out_specs=(pl.BlockSpec(memory_space=pltpu.VMEM),) * 2,
        scratch_shapes=[
            pltpu.VMEM((width, width), jnp.float32),
            pltpu.VMEM((width, rank), jnp.float32),
            pltpu.VMEM((width, rank), jnp.float32),
            pltpu.VMEM((BLOCK, 2 * BLOCK), jnp.float32),
        ],
        compiler_params=pltpu.CompilerParams(vmem_limit_bytes=48 * 2**20),
        name="chain",
    )(packed)


def basis_kernel(together, picks, pieces, *refs):
    weights, out = refs[:together], refs[together]
    rank = out.shape[1]
    for k, weight in enumerate(weights):
        both = lax.dot_general(weight[0], pieces[...], (((0,), (0,)), ((), ())), preferred_element_type=jnp.float32)
        out[k * HEAD_OUT:(k + 1) * HEAD_OUT, :] = both[:, :rank] + both[:, rank:]


def back_projected(picks, pieces, weights):
    width = pieces.shape[0]
    rank = pieces.shape[1] // 2
    heads_here = picks.shape[0]
    together = math.gcd(heads_here, 4)
    return pl.pallas_call(
        functools.partial(basis_kernel, together),
        out_shape=jax.ShapeDtypeStruct((heads_here * HEAD_OUT, rank), jnp.float32),
        grid_spec=pltpu.PrefetchScalarGridSpec(
            num_scalar_prefetch=1,
            grid=(heads_here // together,),
            in_specs=[pl.BlockSpec(pieces.shape, lambda at, picks: (0, 0))] + weight_specs(together, width),
            out_specs=pl.BlockSpec((together * HEAD_OUT, rank), lambda at, picks: (at, 0)),
        ),
        compiler_params=pltpu.CompilerParams(vmem_limit_bytes=48 * 2**20),
        name="back_projected",
    )(picks, pieces, *[weights] * together)


def on_device(latents, weights, start_basis, layer_pick):
    act = latents[0]
    width = act.shape[1]
    rank = start_basis.shape[1]
    heads_here = weights.shape[2] // HEAD_OUT
    slot = lax.axis_index("col")
    first_head = lax.axis_index(("tok", "head")) * heads_here
    picks = lax.dynamic_slice(layer_pick, (slot, first_head), (1, heads_here))[0]
    unit = 16 * lax.axis_size("tok")
    rows = -(-(width + 4 * HALF + 2) // unit) * unit
    packed = summed(local_sums(picks, act, start_basis, weights, rows))
    core, pieces = chain(packed, width, rank)
    return (back_projected(picks, pieces, weights)[None], core[None])


def solution(mesh):
    return jax.shard_map(
        on_device,
        mesh=mesh,
        in_specs=(
            P(("groups", "col"), ("tok", "head"), None),
            P(None, None, ("tok", "head")),
            P(("tok", "head"), None),
            P("groups", None),
        ),
        out_specs=(P(("groups", "col"), ("tok", "head"), None), P(("groups", "col"), None, None)),
        check_vma=False,
    )
```

time: 641 us -> 110 us (0.17)
  the two profiles are of different devices: /device:TPU:0 before, /device:TPU:25 now
where the time goes in v2:
time: 110 us
  Pallas kernels  105 us (95%)
  local copies, waits for them, and re-layouts  3.56 us (3%)
    pallas_call x1, Pallas kernels, chain(): pl.pallas_call(chain_kernel, out_shape=(jax.ShapeDtypeStruct((width, rank...  47.6 us
    pallas_call x1, Pallas kernels, summed(): pl.pallas_call(functools.partial(sum_kernel, count), out_shape=jax.ShapeD...  44.1 us
    pallas_call x1, Pallas kernels, local_sums(): pl.pallas_call(functools.partial(local_sums_kernel, together), out_shape=...  7.01 us
    pallas_call x1, Pallas kernels, back_projected(): pl.pallas_call(functools.partial(basis_kernel, together), out_shape=jax.S...  6.75 us
    unnamed x6, local copies, waits for them, and re-layouts  3.48 us

profile of v2, /device:TPU:25, one launch (start us, length us, event | category | flops | bytes accessed | tf_op | source)
XLA Modules:
  0.0 109.7 jit_solution(8884703350030115066)
XLA Ops:
  0.6 0.0 copy-start
  0.7 0.7 copy-done
  1.3 0.1 dynamic-slice_bitcast_fusion.picks
  1.4 0.0 copy-start.1
  1.4 1.6 %copy-done.1 = bf16[4096,256]{1,0:T(8,128)(2,1)S(1)} copy-done((bf16[4096,256]{1,0:T(8,128)(2,1)S(1)}, bf16[4096,256]{1,0:T(8,128)(2,1)}, u32[]{:S(2)}) %copy-start.1) | copy-done | bytes 2097176
  3.0 0.0 copy-start.2
  3.0 1.2 %copy-done.2 = bf16[1,1024,512]{2,1,0:T(8,128)(2,1)S(1)} copy-done((bf16[1,1024,512]{2,1,0:T(8,128)(2,1)S(1)}, bf16[1,1024,512]{2,1,0:T(8,128)(2,1)}, u32[]{:S(2)}) %copy-start.2) | copy-done | bytes 1048600
  4.2 7.0 %local_sums.1.x = f32[1600,256]{1,0:T(8,128)S(1)} custom-call(s32[16]{0:T(128)S(1)} %dynamic-slice_bitcast_fusion.picks, bf16[1024,512]{1,0:T(8,128)(2,1)S(1)} %bitcast.5, bf16[4096,256]{1,0:T(8,128)(2,1)S(1)} %copy-done.1, bf16[2,512,4096]{2,1,0:T(8,128)(2,1)} %refs_3_.3, bf16[2,512,4096]{2,1,0:T(8,128)(2,1)} %refs_3_.3, bf16[2,512,4096]{2,1,0:T(8,128)(2,1)} %refs_3_.3, ...), custom_call_target="tpu_custom_call" | custom-call | tf_op jit(solution)/shard_map/local_sums/pallas_call | solution.py:64
  11.2 44.1 %summed.1.packed = f32[1600,256]{1,0:T(8,128)S(1)} custom-call(f32[1600,256]{1,0:T(8,128)S(1)} %local_sums.1.x), custom_call_target="tpu_custom_call" | custom-call | tf_op jit(solution)/shard_map/summed/pallas_call | solution.py:146
  55.3 47.6 %chain.1 = (f32[512,256]{1,0:T(8,128)}, bf16[512,512]{1,0:T(8,128)(2,1)S(1)}) custom-call(f32[1600,256]{1,0:T(8,128)S(1)} %summed.1.packed), custom_call_target="tpu_custom_call" | custom-call | tf_op jit(solution)/shard_map/chain/pallas_call | solution.py:260
  102.9 6.7 %back_projected.1 = f32[4096,256]{1,0:T(8,128)} custom-call(s32[16]{0:T(128)S(1)} %dynamic-slice_bitcast_fusion.picks, bf16[512,512]{1,0:T(8,128)(2,1)S(1)} %get-tuple-element.4.pieces, bf16[2,512,4096]{2,1,0:T(8,128)(2,1)} %refs_3_.3, bf16[2,512,4096]{2,1,0:T(8,128)(2,1)} %refs_3_.3, bf16[2,512,4096]{2,1,0:T(8,128)(2,1)} %refs_3_.3, ...), custom_call_target="tpu_custom_call" | custom-call | tf_op jit(solution)/shard_map/back_projected/pallas_call | solution.py:289
Async XLA Ops:
  0.6 0.7 copy-start
  1.4 1.6 %copy-start.1 = (bf16[4096,256]{1,0:T(8,128)(2,1)S(1)}, bf16[4096,256]{1,0:T(8,128)(2,1)}, u32[]{:S(2)}) copy-start(bf16[4096,256]{1,0:T(8,128)(2,1)} %start.1) | copy-start | bytes 6291460
  3.0 1.2 %copy-start.2 = (bf16[1,1024,512]{2,1,0:T(8,128)(2,1)S(1)}, bf16[1,1024,512]{2,1,0:T(8,128)(2,1)}, u32[]{:S(2)}) copy-start(bf16[1,1024,512]{2,1,0:T(8,128)(2,1)} %param.4) | copy-start | bytes 3145732

commit v3 on v2

--- a/solution.py
+++ b/solution.py
@@ -14,6 +14,7 @@
 HALF = 256
 PANEL = 8
 BLOCK = 128
+CHUNKS = 10
 MESH = pl.DeviceIdType.MESH
 
 
@@ -79,76 +80,135 @@
     )(picks, act, start, *[weights] * together)
 
 
-def sum_kernel(count, x, out, from_core, chip_sum, from_chips, sems):
+def sum_kernel(count, x, out, from_core, chip_sum, from_back, sems):
     me = lax.axis_index("tok")
     core = lax.axis_index("head")
     half = x.shape[0] // 2
-    shard = half // count
+    chunk = half // CHUNKS
     mine = core * half
     theirs = (1 - core) * half
     partner = {"head": 1 - core}
-
-    def remote(source, target, stage, slot, device):
+    place = jnp.where(core == 0, me, count - 1 - me)
+    ahead = {"tok": jnp.where(core == 0, me + 1, me - 1)}
+    behind = {"tok": jnp.where(core == 0, me - 1, me + 1)}
+    is_first = place == 0
+    is_last = place == count - 1
+
+    def remote(source, target, stage, k, device):
         return pltpu.make_async_remote_copy(
-            src_ref=source, dst_ref=target, send_sem=sems.at[stage, 0, slot], recv_sem=sems.at[stage, 1, slot],
+            src_ref=source, dst_ref=target, send_sem=sems.at[stage, 0, k], recv_sem=sems.at[stage, 1, k],
             device_id=device, device_id_type=MESH)
 
-    def rows_of(base, index):
-        return pl.ds(pl.multiple_of(base + index * shard, 8), shard)
-
-    peers = [lax.rem(me + d, count) for d in range(count)]
+    def rows_of(base, k):
+        return pl.ds(pl.multiple_of(base + k * chunk, 8), chunk)
+
+    def to_core(k):
+        return remote(x.at[rows_of(theirs, k)], from_core.at[k], 0, k, partner)
+
+    def onward(k):
+        return remote(chip_sum.at[k], from_back.at[k], 1, k, ahead)
+
+    def returned(k):
+        rows = rows_of(mine, k)
+        return remote(out.at[rows], out.at[rows], 2, k, behind)
+
+    def shared(k):
+        rows = rows_of(mine, k)
+        return remote(out.at[rows], out.at[rows], 3, k, partner)
+
     barrier = pltpu.get_barrier_semaphore()
     pl.semaphore_signal(barrier, inc=1, device_id=partner, device_id_type=MESH)
-    for d in range(1, count):
-        pl.semaphore_signal(barrier, inc=1, device_id={"tok": peers[d]}, device_id_type=MESH)
-    pl.semaphore_wait(barrier, count)
-
-    order = list(range(1, count)) + [0]
-    first = [remote(x.at[rows_of(theirs, peers[d])], from_core.at[d], 0, d, partner) for d in range(count)]
-    for d in order:
-        first[d].start()
-    second = [None] + [remote(chip_sum.at[d], from_chips.at[d], 1, d, {"tok": peers[d]}) for d in range(1, count)]
-    for d in order:
-        first[d].wait_recv()
-        chip_sum[d] = x[rows_of(mine, peers[d]), :] + from_core[d]
-        if d:
-            second[d].start()
-    total = chip_sum[0]
-    for d in range(1, count):
-        second[d].wait_recv()
-        total = total + from_chips[d]
-    own = rows_of(mine, me)
-    out[own, :] = total
-    third = [remote(out.at[own], out.at[own], 2, d, {"tok": peers[d]} if d else partner) for d in range(count)]
-    for d in order:
-        third[d].start()
-    fourth = [None]
-    for d in range(1, count):
-        third[d].wait_recv()
-        source = out.at[rows_of(mine, lax.rem(me - d + count, count))]
-        fourth.append(remote(source, source, 3, d, partner))
-        fourth[d].start()
-    third[0].wait_recv()
-    for d in range(1, count):
-        fourth[d].wait_recv()
-    for d in range(count):
-        first[d].wait_send()
-        third[d].wait_send()
-        if d:
-            second[d].wait_send()
-            fourth[d].wait_send()
+
+    @pl.when(jnp.logical_not(is_first))
+    def _():
+        pl.semaphore_signal(barrier, inc=1, device_id=behind, device_id_type=MESH)
+
+    @pl.when(jnp.logical_not(is_last))
+    def _():
+        pl.semaphore_signal(barrier, inc=1, device_id=ahead, device_id_type=MESH)
+
+    at_end = jnp.logical_or(is_first, is_last)
+
+    @pl.when(at_end)
+    def _():
+        pl.semaphore_wait(barrier, 2)
+
+    @pl.when(jnp.logical_not(at_end))
+    def _():
+        pl.semaphore_wait(barrier, 3)
+
+    def start(k, carry):
+        to_core(k).start()
+        return carry
+
+    lax.fori_loop(0, CHUNKS, start, 0)
+    lag = 2 * (count - 1 - place)
+
+    def body(i, carry):
+        @pl.when(i < CHUNKS)
+        def _():
+            to_core(i).wait_recv()
+            chip_sum[i] = x[rows_of(mine, i), :] + from_core[i]
+
+            @pl.when(jnp.logical_not(is_first))
+            def _():
+                onward(i).wait_recv()
+                chip_sum[i] = chip_sum[i] + from_back[i]
+
+            @pl.when(jnp.logical_not(is_last))
+            def _():
+                onward(i).start()
+
+            @pl.when(is_last)
+            def _():
+                out[rows_of(mine, i), :] = chip_sum[i]
+
+        k = i - lag
+
+        @pl.when(jnp.logical_and(k >= 0, k < CHUNKS))
+        def _():
+            @pl.when(jnp.logical_not(is_last))
+            def _():
+                returned(k).wait_recv()
+
+            @pl.when(jnp.logical_not(is_first))
+            def _():
+                returned(k).start()
+
+            shared(k).start()
+
+        return carry
+
+    lax.fori_loop(0, CHUNKS + 2 * (count - 1), body, 0)
+
+    def finish(k, carry):
+        shared(k).wait_recv()
+        shared(k).wait_send()
+        to_core(k).wait_send()
+
+        @pl.when(jnp.logical_not(is_last))
+        def _():
+            onward(k).wait_send()
+
+        @pl.when(jnp.logical_not(is_first))
+        def _():
+            returned(k).wait_send()
+
+        return carry
+
+    lax.fori_loop(0, CHUNKS, finish, 0)
 
 
 def summed(x):
     count = lax.axis_size("tok")
-    shard = x.shape[0] // 2 // count
-    slots = pltpu.VMEM((count, shard, x.shape[1]), jnp.float32)
+    chunk = x.shape[0] // 2 // CHUNKS
+    slots = pltpu.VMEM((CHUNKS, chunk, x.shape[1]), jnp.float32)
     return pl.pallas_call(
         functools.partial(sum_kernel, count),
         out_shape=jax.ShapeDtypeStruct(x.shape, jnp.float32),
         in_specs=[pl.BlockSpec(memory_space=pltpu.VMEM)],
         out_specs=pl.BlockSpec(memory_space=pltpu.VMEM),
-        scratch_shapes=[slots, slots, slots, pltpu.SemaphoreType.DMA((4, 2, count))],
+        scratch_shapes=[slots, slots, slots, pltpu.SemaphoreType.DMA((4, 2, CHUNKS))],
         compiler_params=pltpu.CompilerParams(collective_id=0, has_side_effects=True, vmem_limit_bytes=48 * 2**20),
         name="summed",
     )(x)
@@ -157,6 +217,16 @@
 def exact_dot(left, right, contract=(1, 0)):
     dims = (((contract[0],), (contract[1],)), ((), ()))
     return lax.dot_general(left, right, dims, precision=lax.Precision.HIGHEST, preferred_element_type=jnp.float32)
+
+
+def stacked_dot(rows, size):
+    high = rows.astype(jnp.bfloat16).astype(jnp.float32)
+    rest = rows - high
+    middle = rest.astype(jnp.bfloat16).astype(jnp.float32)
+    low = rest - middle
+    left = jnp.concatenate([p[:, :size] for p in (high, high, middle, high, low, middle)], axis=0).astype(jnp.bfloat16)
+    right = jnp.concatenate([high, middle, high, low, high, middle], axis=0).astype(jnp.bfloat16)
+    return lax.dot_general(left, right, (((0,), (0,)), ((), ())), preferred_element_type=jnp.float32)
 
 
 def inverse_factor(work, size):
@@ -180,7 +250,7 @@
         work[first:first + PANEL, :] = rows
         rest = first + PANEL
         if rest < size:
-            update = exact_dot(rows[:, :size], rows, (0, 0))
+            update = stacked_dot(rows, size)
             work[rest:, :] = work[rest:, :] - update[rest:, :]
     return work[:, size:]
 
@@ -308,7 +378,7 @@
     slot = lax.axis_index("col")
     first_head = lax.axis_index(("tok", "head")) * heads_here
     picks = lax.dynamic_slice(layer_pick, (slot, first_head), (1, heads_here))[0]
-    unit = 16 * lax.axis_size("tok")
+    unit = 16 * CHUNKS
     rows = -(-(width + 4 * HALF + 2) // unit) * unit
     packed = summed(local_sums(picks, act, start_basis, weights, rows))
     core, pieces = chain(packed, width, rank)

time: 110 us -> 106 us (0.964)
  the two profiles are of different devices: /device:TPU:25 before, /device:TPU:0 now
where the time goes in v3:
time: 106 us
  Pallas kernels  101 us (95%)
  local copies, waits for them, and re-layouts  3.56 us (3%)
    pallas_call x1, Pallas kernels, summed(): pl.pallas_call(functools.partial(sum_kernel, count), out_shape=jax.ShapeD...  51.3 us
    pallas_call x1, Pallas kernels, chain(): pl.pallas_call(chain_kernel, out_shape=(jax.ShapeDtypeStruct((width, rank...  36.4 us
    pallas_call x1, Pallas kernels, local_sums(): pl.pallas_call(functools.partial(local_sums_kernel, together), out_shape=...  6.99 us
    pallas_call x1, Pallas kernels, back_projected(): pl.pallas_call(functools.partial(basis_kernel, together), out_shape=jax.S...  6.75 us
    unnamed x6, local copies, waits for them, and re-layouts  3.48 us

profile of v3, /device:TPU:0, one launch (start us, length us, event | category | flops | bytes accessed | tf_op | source)
XLA Modules:
  0.0 105.7 jit_solution(14013272364274971705)
XLA Ops:
  0.6 0.0 copy-start
  0.7 0.7 copy-done
  1.3 0.1 dynamic-slice_bitcast_fusion.picks
  1.4 0.0 copy-start.1
  1.4 1.6 %copy-done.1 = bf16[4096,256]{1,0:T(8,128)(2,1)S(1)} copy-done((bf16[4096,256]{1,0:T(8,128)(2,1)S(1)}, bf16[4096,256]{1,0:T(8,128)(2,1)}, u32[]{:S(2)}) %copy-start.1) | copy-done | bytes 2097176
  3.0 0.0 copy-start.2
  3.0 1.2 %copy-done.2 = bf16[1,1024,512]{2,1,0:T(8,128)(2,1)S(1)} copy-done((bf16[1,1024,512]{2,1,0:T(8,128)(2,1)S(1)}, bf16[1,1024,512]{2,1,0:T(8,128)(2,1)}, u32[]{:S(2)}) %copy-start.2) | copy-done | bytes 1048600
  4.2 7.0 %local_sums.1.x = f32[1600,256]{1,0:T(8,128)S(1)} custom-call(s32[16]{0:T(128)S(1)} %dynamic-slice_bitcast_fusion.picks, bf16[1024,512]{1,0:T(8,128)(2,1)S(1)} %bitcast.5, bf16[4096,256]{1,0:T(8,128)(2,1)S(1)} %copy-done.1, bf16[2,512,4096]{2,1,0:T(8,128)(2,1)} %refs_3_.3, bf16[2,512,4096]{2,1,0:T(8,128)(2,1)} %refs_3_.3, bf16[2,512,4096]{2,1,0:T(8,128)(2,1)} %refs_3_.3, ...), custom_call_target="tpu_custom_call" | custom-call | tf_op jit(solution)/shard_map/local_sums/pallas_call | solution.py:65
  11.2 51.3 %summed.1.packed = f32[1600,256]{1,0:T(8,128)S(1)} custom-call(f32[1600,256]{1,0:T(8,128)S(1)} %local_sums.1.x), custom_call_target="tpu_custom_call" | custom-call | tf_op jit(solution)/shard_map/summed/pallas_call | solution.py:206
  62.5 36.4 %chain.1 = (f32[512,256]{1,0:T(8,128)}, bf16[512,512]{1,0:T(8,128)(2,1)S(1)}) custom-call(f32[1600,256]{1,0:T(8,128)S(1)} %summed.1.packed), custom_call_target="tpu_custom_call" | custom-call | tf_op jit(solution)/shard_map/chain/pallas_call | solution.py:330
  99.0 6.8 %back_projected.1 = f32[4096,256]{1,0:T(8,128)} custom-call(s32[16]{0:T(128)S(1)} %dynamic-slice_bitcast_fusion.picks, bf16[512,512]{1,0:T(8,128)(2,1)S(1)} %get-tuple-element.4.pieces, bf16[2,512,4096]{2,1,0:T(8,128)(2,1)} %refs_3_.3, bf16[2,512,4096]{2,1,0:T(8,128)(2,1)} %refs_3_.3, bf16[2,512,4096]{2,1,0:T(8,128)(2,1)} %refs_3_.3, ...), custom_call_target="tpu_custom_call" | custom-call | tf_op jit(solution)/shard_map/back_projected/pallas_call | solution.py:359
Async XLA Ops:
  0.6 0.7 copy-start
  1.4 1.6 %copy-start.1 = (bf16[4096,256]{1,0:T(8,128)(2,1)S(1)}, bf16[4096,256]{1,0:T(8,128)(2,1)}, u32[]{:S(2)}) copy-start(bf16[4096,256]{1,0:T(8,128)(2,1)} %start.1) | copy-start | bytes 6291460
  3.0 1.2 %copy-start.2 = (bf16[1,1024,512]{2,1,0:T(8,128)(2,1)S(1)}, bf16[1,1024,512]{2,1,0:T(8,128)(2,1)}, u32[]{:S(2)}) copy-start(bf16[1,1024,512]{2,1,0:T(8,128)(2,1)} %param.4) | copy-start | bytes 3145732

commit v4 on v2

--- a/solution.py
+++ b/solution.py
@@ -159,30 +159,50 @@
     return lax.dot_general(left, right, dims, precision=lax.Precision.HIGHEST, preferred_element_type=jnp.float32)
 
 
-def inverse_factor(work, size):
-    sublane = lax.broadcasted_iota(jnp.int32, (PANEL, 2 * size), 0)
+def stacked_dot(rows, size):
+    high = rows.astype(jnp.bfloat16).astype(jnp.float32)
+    rest = rows - high
+    middle = rest.astype(jnp.bfloat16).astype(jnp.float32)
+    low = rest - middle
+    left = jnp.concatenate([p[:, :size] for p in (high, high, middle, high, low, middle)], axis=0).astype(jnp.bfloat16)
+    right = jnp.concatenate([high, middle, high, low, high, middle], axis=0).astype(jnp.bfloat16)
+    return lax.dot_general(left, right, (((0,), (0,)), ((), ())), preferred_element_type=jnp.float32)
+
+
+def eliminate_panel(work, size, first):
+    sublane = lax.broadcasted_iota(jnp.int32, (PANEL, 128), 0)
+    rows = work[first:first + PANEL, :]
+    columns = [jnp.broadcast_to(rows[:, first + c:first + c + 1], (PANEL, 128)) for c in range(PANEL)]
+    scale = jnp.zeros((PANEL, 128), jnp.float32)
+    for c in range(PANEL):
+        pivot = jnp.broadcast_to(columns[c][c:c + 1, :], (PANEL, 128))
+        scale = jnp.where(sublane == c, pivot, scale)
+        if c == PANEL - 1:
+            break
+        factor = jnp.where(sublane > c, columns[c] / pivot, 0.0)
+        for later in range(c + 1, PANEL):
+            columns[later] = columns[later] - factor * columns[later][c:c + 1, :]
+        wide = jnp.concatenate([factor] * (2 * size // 128), axis=1)
+        rows = rows - wide * rows[c:c + 1, :]
+    inverse_root = lax.rsqrt(scale)
+    rows = rows * jnp.concatenate([inverse_root] * (2 * size // 128), axis=1)
+    work[first:first + PANEL, :] = rows
+    rest = first + PANEL
+    if rest < size:
+        work[rest:, :] = work[rest:, :] - stacked_dot(rows, size)[rest:, :]
+
+
+def inverse_factors(works, blocks):
+    size = blocks[0].shape[0]
+    row = lax.broadcasted_iota(jnp.int32, (size, size), 0)
+    column = lax.broadcasted_iota(jnp.int32, (size, size), 1)
+    for work, block in zip(works, blocks):
+        work[:, :size] = block
+        work[:, size:] = (row == column).astype(jnp.float32)
     for first in range(0, size, PANEL):
-        rows = work[first:first + PANEL, :]
-        columns = [jnp.broadcast_to(rows[:, first + c:first + c + 1], (PANEL, 128)) for c in range(PANEL)]
-        scale = jnp.zeros((PANEL, 128), jnp.float32)
-        for c in range(PANEL):
-            pivot = jnp.broadcast_to(columns[c][c:c + 1, :], (PANEL, 128))
-            scale = jnp.where(sublane[:, :128] == c, pivot, scale)
-            if c == PANEL - 1:
-                break
-            factor = jnp.where(sublane[:, :128] > c, columns[c] / pivot, 0.0)
-            for later in range(c + 1, PANEL):
-                columns[later] = columns[later] - factor * columns[later][c:c + 1, :]
-            wide = jnp.concatenate([factor] * (2 * size // 128), axis=1)
-            rows = rows - wide * rows[c:c + 1, :]
-        inverse_root = lax.rsqrt(scale)
-        rows = rows * jnp.concatenate([inverse_root] * (2 * size // 128), axis=1)
-        work[first:first + PANEL, :] = rows
-        rest = first + PANEL
-        if rest < size:
-            update = exact_dot(rows[:, :size], rows, (0, 0))
-            work[rest:, :] = work[rest:, :] - update[rest:, :]
-    return work[:, size:]
+        for work, _ in zip(works, blocks):
+            eliminate_panel(work, size, first)
+    return [jnp.where(row >= column, work[:, size:], 0.0) for work, _ in zip(works, blocks)]
 
 
 def unpacked(packed, first, diagonal):
@@ -200,7 +220,51 @@
     ], axis=0)
 
 
-def chain_kernel(packed, image_out, pieces_out, weight_gram_ref, image_work, back_work, work):
+def blocks_of(square):
+    count = square.shape[0] // BLOCK
+    return {(i, j): square[i * BLOCK:(i + 1) * BLOCK, j * BLOCK:(j + 1) * BLOCK] for i in range(count) for j in range(i + 1)}
+
+
+def conditioned(works, back, mixed, square):
+    blocks = blocks_of(square)
+    count = square.shape[0] // BLOCK
+    inverses = inverse_factors(works, [blocks[i, i] for i in range(count)])
+    done = []
+    for i, inverse in enumerate(inverses):
+        here = slice(i * BLOCK, (i + 1) * BLOCK)
+        part_back = exact_dot(back[:, here], inverse, (1, 1))
+        part_mixed = exact_dot(mixed[:, here], inverse, (1, 1))
+        for before_back, before_mixed in done:
+            shared = exact_dot(before_back, part_mixed, (0, 0))
+            part_back = part_back - exact_dot(before_back, shared)
+            part_mixed = part_mixed - exact_dot(before_mixed, shared)
+        done.append((part_back, part_mixed))
+    return done
+
+
+def orthonormal(works, back, mixed, square):
+    schur = blocks_of(square)
+    count = square.shape[0] // BLOCK
+    below = {}
+    done = []
+    for i in range(count):
+        here = slice(i * BLOCK, (i + 1) * BLOCK)
+        inverse, = inverse_factors(works[:1], [schur[i, i]])
+        part_back = back[:, here]
+        part_mixed = mixed[:, here]
+        for j in range(i):
+            part_back = part_back - exact_dot(done[j][0], below[i, j], (1, 1))
+            part_mixed = part_mixed - exact_dot(done[j][1], below[i, j], (1, 1))
+        done.append((exact_dot(part_back, inverse, (1, 1)), exact_dot(part_mixed, inverse, (1, 1))))
+        for k in range(i + 1, count):
+            below[k, i] = exact_dot(schur[k, i], inverse, (1, 1))
+        for k in range(i + 1, count):
+            for m in range(i + 1, k + 1):
+                schur[k, m] = schur[k, m] - exact_dot(below[k, i], below[m, i], (1, 1))
+    return done
+
+
+def chain_kernel(packed, image_out, pieces_out, weight_gram_ref, image_work, back_work, *works):
     width, rank = image_work.shape
     row = lax.broadcasted_iota(jnp.int32, (width, width), 0)
     column = lax.broadcasted_iota(jnp.int32, (width, width), 1)
@@ -209,46 +273,13 @@
     weight_gram_ref[...] = unpacked(packed, width + 2 * HALF, width + 4 * HALF + 1)
     image = packed[:width, :]
     image_work[...] = image / jnp.sqrt(jnp.mean(image * image))
-    eye = (row[:BLOCK, :BLOCK] == column[:BLOCK, :BLOCK]).astype(jnp.float32)
-
-    def step(_, carry):
+    for step in range(STEPS):
         back = exact_dot(gram, image_work[...])
         mixed = exact_dot(weight_gram_ref[...], back)
         square = exact_dot(back, mixed, (0, 0))
-        pieces = []
-        count = rank // BLOCK
-        schur = {}
-        for i in range(count):
-            for j in range(i + 1):
-                schur[i, j] = square[i * BLOCK:(i + 1) * BLOCK, j * BLOCK:(j + 1) * BLOCK]
-        inverse = []
-        below = {}
-        done = []
-        for i in range(count):
-            current = schur[i, i]
-            work[:, :BLOCK] = current
-            work[:, BLOCK:] = eye
-            inv = inverse_factor(work, BLOCK)
-            lower_mask = row[:BLOCK, :BLOCK] >= column[:BLOCK, :BLOCK]
-            inv = jnp.where(lower_mask, inv, 0.0)
-            part_back = back[:, i * BLOCK:(i + 1) * BLOCK]
-            part_mixed = mixed[:, i * BLOCK:(i + 1) * BLOCK]
-            for j in range(i):
-                part_back = part_back - exact_dot(done[j][0], below[i, j], (1, 1))
-                part_mixed = part_mixed - exact_dot(done[j][1], below[i, j], (1, 1))
-            part_back = exact_dot(part_back, inv, (1, 1))
-            part_mixed = exact_dot(part_mixed, inv, (1, 1))
-            done.append((part_back, part_mixed))
-            for k in range(i + 1, count):
-                below[k, i] = exact_dot(schur[k, i], inv, (1, 1))
-            for k in range(i + 1, count):
-                for m in range(i + 1, k + 1):
-                    schur[k, m] = schur[k, m] - exact_dot(below[k, i], below[m, i], (1, 1))
-        back_work[...] = jnp.concatenate([d[0] for d in done], axis=1)
+        done = (orthonormal if step == STEPS - 1 else conditioned)(works, back, mixed, square)
         image_work[...] = jnp.concatenate([d[1] for d in done], axis=1)
-        return carry
-
-    lax.fori_loop(0, STEPS, step, 0)
+    back_work[...] = jnp.concatenate([d[0] for d in done], axis=1)
     image_out[...] = image_work[...]
     scaled = back_work[...] * math.sqrt(OUT)
     high = scaled.astype(jnp.bfloat16)
@@ -266,8 +297,7 @@
             pltpu.VMEM((width, width), jnp.float32),
             pltpu.VMEM((width, rank), jnp.float32),
             pltpu.VMEM((width, rank), jnp.float32),
-            pltpu.VMEM((BLOCK, 2 * BLOCK), jnp.float32),
-        ],
+        ] + [pltpu.VMEM((BLOCK, 2 * BLOCK), jnp.float32)] * (rank // BLOCK),
         compiler_params=pltpu.CompilerParams(vmem_limit_bytes=48 * 2**20),
         name="chain",
     )(packed)

time: 110 us -> 93.6 us (0.85)
  the two profiles are of different devices: /device:TPU:25 before, /device:TPU:27 now
where the time goes in v4:
time: 93.6 us; the launch traced here: 93.2 us
  Pallas kernels  89 us (95%)
  local copies, waits for them, and re-layouts  3.56 us (4%)
    pallas_call x1, Pallas kernels, summed(): pl.pallas_call(functools.partial(sum_kernel, count), out_shape=jax.ShapeD...  44.1 us
    pallas_call x1, Pallas kernels, chain(): pl.pallas_call(chain_kernel, out_shape=(jax.ShapeDtypeStruct((width, rank...  31.1 us
    pallas_call x1, Pallas kernels, local_sums(): pl.pallas_call(functools.partial(local_sums_kernel, together), out_shape=...  6.99 us
    pallas_call x1, Pallas kernels, back_projected(): pl.pallas_call(functools.partial(basis_kernel, together), out_shape=jax.S...  6.75 us
    unnamed x6, local copies, waits for them, and re-layouts  3.48 us

profile of v4, /device:TPU:27, one launch (start us, length us, event | category | flops | bytes accessed | tf_op | source)
XLA Modules:
  0.0 93.2 jit_solution(5863430204225697054)
XLA Ops:
  0.6 0.0 copy-start
  0.7 0.7 copy-done
  1.3 0.1 dynamic-slice_bitcast_fusion.picks
  1.4 0.0 copy-start.1
  1.4 1.6 %copy-done.1 = bf16[4096,256]{1,0:T(8,128)(2,1)S(1)} copy-done((bf16[4096,256]{1,0:T(8,128)(2,1)S(1)}, bf16[4096,256]{1,0:T(8,128)(2,1)}, u32[]{:S(2)}) %copy-start.1) | copy-done | bytes 2097176
  3.0 0.0 copy-start.2
  3.0 1.2 %copy-done.2 = bf16[1,1024,512]{2,1,0:T(8,128)(2,1)S(1)} copy-done((bf16[1,1024,512]{2,1,0:T(8,128)(2,1)S(1)}, bf16[1,1024,512]{2,1,0:T(8,128)(2,1)}, u32[]{:S(2)}) %copy-start.2) | copy-done | bytes 1048600
  4.2 7.0 %local_sums.1.x = f32[1600,256]{1,0:T(8,128)S(1)} custom-call(s32[16]{0:T(128)S(1)} %dynamic-slice_bitcast_fusion.picks, bf16[1024,512]{1,0:T(8,128)(2,1)S(1)} %bitcast.5, bf16[4096,256]{1,0:T(8,128)(2,1)S(1)} %copy-done.1, bf16[2,512,4096]{2,1,0:T(8,128)(2,1)} %refs_3_.3, bf16[2,512,4096]{2,1,0:T(8,128)(2,1)} %refs_3_.3, bf16[2,512,4096]{2,1,0:T(8,128)(2,1)} %refs_3_.3, ...), custom_call_target="tpu_custom_call" | custom-call | tf_op jit(solution)/shard_map/local_sums/pallas_call | solution.py:64
  11.2 44.1 %summed.1.packed = f32[1600,256]{1,0:T(8,128)S(1)} custom-call(f32[1600,256]{1,0:T(8,128)S(1)} %local_sums.1.x), custom_call_target="tpu_custom_call" | custom-call | tf_op jit(solution)/shard_map/summed/pallas_call | solution.py:146
  55.4 31.1 %chain.1 = (f32[512,256]{1,0:T(8,128)}, bf16[512,512]{1,0:T(8,128)(2,1)S(1)}) custom-call(f32[1600,256]{1,0:T(8,128)S(1)} %summed.1.packed), custom_call_target="tpu_custom_call" | custom-call | tf_op jit(solution)/shard_map/chain/pallas_call | solution.py:291
  86.5 6.8 %back_projected.1 = f32[4096,256]{1,0:T(8,128)} custom-call(s32[16]{0:T(128)S(1)} %dynamic-slice_bitcast_fusion.picks, bf16[512,512]{1,0:T(8,128)(2,1)S(1)} %get-tuple-element.4.pieces, bf16[2,512,4096]{2,1,0:T(8,128)(2,1)} %refs_3_.3, bf16[2,512,4096]{2,1,0:T(8,128)(2,1)} %refs_3_.3, bf16[2,512,4096]{2,1,0:T(8,128)(2,1)} %refs_3_.3, ...), custom_call_target="tpu_custom_call" | custom-call | tf_op jit(solution)/shard_map/back_projected/pallas_call | solution.py:319
Async XLA Ops:
  0.6 0.7 copy-start
  1.4 1.6 %copy-start.1 = (bf16[4096,256]{1,0:T(8,128)(2,1)S(1)}, bf16[4096,256]{1,0:T(8,128)(2,1)}, u32[]{:S(2)}) copy-start(bf16[4096,256]{1,0:T(8,128)(2,1)} %start.1) | copy-start | bytes 6291460
  3.0 1.2 %copy-start.2 = (bf16[1,1024,512]{2,1,0:T(8,128)(2,1)S(1)}, bf16[1,1024,512]{2,1,0:T(8,128)(2,1)}, u32[]{:S(2)}) copy-start(bf16[1,1024,512]{2,1,0:T(8,128)(2,1)} %param.4) | copy-start | bytes 3145732
